TPU v7x, 256 devices: a whole 4x4x8 slice. The times are simulated.
256 devices in a mesh: dp: 2 (over z_lo), fsdp: 128 (over z_hi, x, y, core).
Axes of the slice: x: 4, y: 4, z: 8 (z_hi: 4, z_lo: 2; z = z_hi * 2 + z_lo), core: 2. Of those that a mesh axis runs over, the one named last changes fastest.
Arguments:
- output_gradient: bfloat16 [1024, 16384], P('dp', 'fsdp'), may hold values from -6 to 6
- gate_preactivation: bfloat16 [1024, 32768], P('dp', 'fsdp'), may hold values from -6 to 6
- up_preactivation: bfloat16 [1024, 32768], P('dp', 'fsdp'), may hold values from -6 to 6
- down_packed_codes: int32 [32768, 8192], P('fsdp'), may hold values from 0 to 255
- down_group_scales: float32 [256, 16384], P('fsdp'), may hold values from 0.0002762136 to 0.0022097088
- down_zero_points: int32 [256, 16384], P('fsdp'), may hold values from 0 to 15
- adapter_input_map: bfloat16 [16, 32768], P(None, 'fsdp'), may hold values from -0.5 to 0.5
- adapter_output_map: bfloat16 [16, 16384], P(None, 'fsdp'), may hold values from -0.046875 to 0.046875
Outputs:
- gate_gradient: bfloat16 [1024, 32768], P('dp', 'fsdp')
- up_gradient: bfloat16 [1024, 32768], P('dp', 'fsdp')
- adapter_input_gradient: float32 [16, 32768], P(None, 'fsdp')
- adapter_output_gradient: float32 [16, 16384], P(None, 'fsdp')
Inputs may be any that keep to these rules, and one draw needn't show every extreme that they name: `down_packed_codes`: each word holds the code of feature d in bits 0 to 3 and that of feature d + 8192 in bits 4 to 7.
All inputs are finite; a program needn't handle non-finite values.
Results may differ from a plain program's by a relative error of at most 0.0051.
Values may be sent and summed in bfloat16 or wider, within the bound.
A program may use at most 128 MiB of HBM per device.

v0:
```python
import jax
import jax.numpy as jnp
from jax import lax
from jax.sharding import PartitionSpec as P

adapter_scale = 2.0


def dequantize(codes, scales, zeros, group):
    rows = codes.shape[0]
    half = codes.shape[1]
    lower = jnp.bitwise_and(codes, 15)
    upper = jnp.bitwise_and(jnp.right_shift(codes, 4), 15)
    levels = jnp.concatenate([lower, upper], axis=1).reshape(rows // group, group, 2 * half)
    values = scales[:, None, :] * (levels - zeros[:, None, :]).astype(jnp.float32)
    return values.reshape(rows, 2 * half).astype(jnp.bfloat16)


def local(
    output_gradient,
    gate_preactivation,
    up_preactivation,
    down_packed_codes,
    down_group_scales,
    down_zero_points,
    adapter_input_map,
    adapter_output_map,
):
    group = down_packed_codes.shape[0] // down_group_scales.shape[0]
    weights = dequantize(down_packed_codes, down_group_scales, down_zero_points, group)
    inner_product = (((1,), (1,)), ((), ()))
    outer = (((0,), (0,)), ((), ()))
    gate_f = gate_preactivation.astype(jnp.float32)
    up_f = up_preactivation.astype(jnp.float32)
    sigma = jax.nn.sigmoid(gate_f)
    hidden_units = (gate_f * sigma * up_f).astype(jnp.bfloat16)
    left_portion = lax.dot_general(
        hidden_units, adapter_input_map, inner_product, preferred_element_type=jnp.float32
    )
    token_row_block = output_gradient.shape[0]
    right_portion = lax.dot_general(
        output_gradient, adapter_output_map, inner_product, preferred_element_type=jnp.float32
    )
    left_full, right_full = lax.psum((left_portion, right_portion), "fsdp")
    frozen_path_gradient = lax.dot_general(
        lax.all_gather(output_gradient, "fsdp", axis=1, tiled=True),
        weights,
        inner_product,
        preferred_element_type=jnp.float32,
    )
    left_lower_nibble = left_full.astype(jnp.bfloat16)
    right_lower_nibble = right_full.astype(jnp.bfloat16)
    hidden_gradient = frozen_path_gradient + adapter_scale * jnp.dot(
        right_lower_nibble, adapter_input_map, preferred_element_type=jnp.float32
    )
    up_gradient = (hidden_gradient * gate_f * sigma).astype(jnp.bfloat16)
    gate_gradient = (hidden_gradient * up_f * sigma * (1.0 + gate_f * (1.0 - sigma))).astype(
        jnp.bfloat16
    )
    scale_factor = adapter_scale / (token_row_block * lax.axis_size("dp"))
    local_adapter_input = scale_factor * lax.dot_general(
        right_lower_nibble, hidden_units, outer, preferred_element_type=jnp.float32
    )
    local_adapter_output = scale_factor * lax.dot_general(
        left_lower_nibble, output_gradient, outer, preferred_element_type=jnp.float32
    )
    adapter_input_gradient, adapter_output_gradient = lax.psum(
        (local_adapter_input, local_adapter_output), "dp"
    )
    return (gate_gradient, up_gradient, adapter_input_gradient, adapter_output_gradient)


def solution(mesh):
    in_specs = (
        P("dp", "fsdp"),
        P("dp", "fsdp"),
        P("dp", "fsdp"),
        P("fsdp", None),
        P("fsdp", None),
        P("fsdp", None),
        P(None, "fsdp"),
        P(None, "fsdp"),
    )
    out_specs = (P("dp", "fsdp"), P("dp", "fsdp"), P(None, "fsdp"), P(None, "fsdp"))
    return jax.shard_map(local, mesh=mesh, in_specs=in_specs, out_specs=out_specs, check_vma=False)
```

profile of v0, /device:TPU:1, one launch (start us, length us, event | category | flops | bytes accessed | tf_op | source)
XLA Modules:
  0.0 763.9 jit_solution(9810198516508303028)
XLA Ops:
  7.2 0.0 copy-start
  7.2 0.0 all-gather.2.cloned.1.call-start
  7.2 0.7 all-gather.2.cloned.1.call-update
  7.9 1.1 copy.14
  9.0 1.1 copy.13
  10.1 0.0 copy-start.2
  10.1 0.0 copy-start.3
  10.1 11.8 %broadcast_and_fusion = (s32[256,8192]{1,0:T(8,128)}, s32[256,8192]{1,0:T(8,128)}) fusion(s32[256,8192]{1,0:T(8,128)} %param.11), kind=kLoop, calls=%fused_computation.5 | loop fusion | flops 6291456 | bytes 25165824 | tf_op jit(solution)/shard_map/and | solution.py:12
  21.9 0.0 copy-done.2
  21.9 0.0 copy-done.3
  22.0 0.0 copy-start.4
  22.0 9.7 %fusion.2 = bf16[256,16384]{1,0:T(8,128)(2,1)} fusion(s32[256,8192]{1,0:T(8,128)} %get-tuple-element.13, s32[256,8192]{1,0:T(8,128)} %get-tuple-element.12, s32[2,16384]{1,0:T(2,128)S(1)} %copy-done.2, f32[2,16384]{1,0:T(2,128)S(1)} %copy-done.3), kind=kLoop, calls=%fused_computation.3 | loop fusion | flops 20971520 | bytes 25427968 | tf_op jit(solution)/shard_map/convert_element_type | solution.py:16
  31.7 0.0 copy-done.1
  31.7 0.1 fusion.17
  31.8 0.2 fusion.7
  32.0 0.3 fusion.18
  32.3 705.7 %all-reduce = (bf16[512,16]{0,1:T(8,128)(2,1)S(1)}, bf16[512,16]{1,0:T(8,128)(2,1)S(1)}) all-reduce(f32[512,16]{0,1:T(8,128)S(1)} %fusion.17, f32[512,16]{1,0:T(8,128)S(1)} %fusion.18), channel_id=1, replica_groups=mesh['dp'=2,'fsdp'=128] {'fsdp'}, use_global_device_ids=true, to_apply=%region_0.0 | all-reduce | flops 16384 | bytes 98304 | tf_op jit(solution)/shard_map/psum | solution.py:44
  738.0 0.2 convolution_multiply_fusion.2
  738.1 0.2 convolution_multiply_fusion.1
  738.3 6.0 all-reduce.1
  744.3 10.5 %convolution_bitcast_fusion = f32[512,256]{0,1:T(8,128)S(1)} fusion(bf16[256,16384]{1,0:T(8,128)(2,1)} %fusion.2, bf16[512,16384]{1,0:T(8,128)(2,1)} %all-gather.2.cloned.1.call-done), kind=kOutput, calls=%fused_computation.8 | convolution fusion | flops 4294967296 | bytes 25690112 | tf_op jit(solution)/shard_map/dot_general | solution.py:45
  754.9 0.5 fusion.13
  755.3 0.8 copy.15
  756.2 0.8 copy.16
  (4 shorter events, 0.0 us)
Async XLA Ops:
  7.2 24.8 %copy-start = (bf16[16,256]{1,0:T(8,128)(2,1)S(1)}, bf16[16,256]{1,0:T(8,128)(2,1)}, u32[]{:S(2)}) copy-start(bf16[16,256]{1,0:T(8,128)(2,1)} %param.14) | copy-start | bytes 24580
  7.2 737.1 %all-gather.2.cloned.1.call-start = ((), (), s32[]{:S(2)}) async-start(), calls=%async_computation | async-start | bytes 16908288 | tf_op jit(solution)/shard_map/all_gather | solution.py:46
  10.1 11.8 %copy-start.2 = (s32[2,16384]{1,0:T(2,128)S(1)}, s32[2,16384]{1,0:T(2,128)}, u32[]{:S(2)}) copy-start(s32[2,16384]{1,0:T(2,128)} %param.13) | copy-start | bytes 393220
  10.1 11.8 %copy-start.3 = (f32[2,16384]{1,0:T(2,128)S(1)}, f32[2,16384]{1,0:T(2,128)}, u32[]{:S(2)}) copy-start(f32[2,16384]{1,0:T(2,128)} %param.12) | copy-start | bytes 393220
  22.0 9.7 %copy-start.1 = (bf16[512,128]{1,0:T(8,128)(2,1)S(1)}, bf16[512,128]{1,0:T(8,128)(2,1)}, u32[]{:S(2)}) copy-start(bf16[512,128]{1,0:T(8,128)(2,1)} %param.8) | copy-start | bytes 393220
  22.0 9.7 %copy-start.4 = (bf16[16,128]{1,0:T(8,128)(2,1)S(1)}, bf16[16,128]{1,0:T(8,128)(2,1)}, u32[]{:S(2)}) copy-start(bf16[16,128]{1,0:T(8,128)(2,1)} %param.15) | copy-start | bytes 12292
Sparse Core Ops, SparseCore 0:
  11.3 155.2 all-gather.1
where the time goes:
time: 773 us; the launch traced here: 764 us
  blocking collectives  712 us (92%)
  other arithmetic  21.7 us (3%)
  between operations  14.1 us (2%)
  matrix products  11.7 us (2%)
    psum x1, blocking collectives, local(): left_full, right_full = lax.psum((left_portion, right_portion), 'fsdp')  706 us
  transfers between devices with their start and end apart: 1, of which 0 were waited for; matrix products, arithmetic and copies ran while one was open for 3% of the time, Pallas kernels for 0%

commit v1 on v0

v1 whole, which is shorter than its diff:
```python
import functools

import jax
import jax.numpy as jnp
from jax import lax
from jax.experimental import pallas as pl
from jax.experimental.pallas import tpu as pltpu
from jax.sharding import PartitionSpec as P

MESH = pl.DeviceIdType.MESH
F32 = jnp.float32
BF16 = jnp.bfloat16
SCALE = 2.0
LAG1, LAG2, LAG_OWN, LAG_SIB = 2, 4, 5, 6
STEPS = 16
NT = (((1,), (1,)), ((), ()))
TN = (((0,), (0,)), ((), ()))


def kernel(
    tokens,
    og, gate, up, codes, scales, zeros, amap, omap,
    gate_out, up_out, ain_out, aout_out,
    buf, w, cbuf, sc_v, ze_v, gate_v, up_v, am_v, om_v, og_v,
    hid, f1, f2, acc, gres, ures,
    p_src, p_dst, r0, s1, s2, s3, s4, fin, ad_mine, ad_peer, ad_sum,
    load_sem, code_sem, local_sem, ssem, sib_ssem, rsem, sib_rsem, own_rsem, small_ssem, small_rsem, out_sem,
):
    dp = lax.axis_index("dp")
    f = lax.axis_index("fsdp")
    c = lax.rem(f, 2)
    y = lax.rem(lax.div(f, 2), 4)
    x = lax.rem(lax.div(f, 8), 4)
    z = lax.div(f, 32)
    a = y + c * (x - y)
    b = x + c * (y - x)
    o = 1 - c

    def chip(px, py, pz, core):
        return (dp, ((pz * 4 + px) * 4 + py) * 2 + core)

    def neighbour(da, dz, db):
        pa, pz, pb = lax.rem(a + da, 4), lax.rem(z + dz, 4), lax.rem(b + db, 4)
        return chip(pb + c * (pa - pb), pa + c * (pb - pa), pz, c)

    sibling = (dp, f + 1 - 2 * c)
    partner = (1 - dp, f)

    def slot(da, dz, db):
        return lax.rem(z + dz, 4) * 16 + lax.rem(a + da, 4) * 4 + lax.rem(b + db, 4)

    def rel(da, dz, db):
        return lax.rem(dz + 4, 4) * 16 + lax.rem(da + 4, 4) * 4 + lax.rem(db + 4, 4)

    def irel(da, dz, db):
        return ((dz % 4) * 4 + da % 4) * 4 + db % 4

    me = slot(0, 0, 0)
    me_other = z * 16 + b * 4 + a

    loads = [
        pltpu.make_async_copy(s, d, load_sem.at[i])
        for i, (s, d) in enumerate(
            ((og, og_v), (gate, gate_v), (up, up_v), (amap, am_v), (omap, om_v), (scales, sc_v), (zeros, ze_v))
        )
    ]
    for load in loads:
        load.start()

    def code_load(ch):
        return pltpu.make_async_copy(
            codes.at[:, pl.ds(pl.multiple_of(ch * 1024, 1024), 1024)], cbuf.at[ch], code_sem.at[ch]
        )

    for ch in range(8):
        code_load(ch).start()

    bar = pltpu.get_barrier_semaphore()
    peers = [neighbour(1, 0, 0), neighbour(2, 0, 0), neighbour(3, 0, 0)]
    peers += [neighbour(0, 1, 0), neighbour(0, 2, 0), neighbour(0, 3, 0)]
    peers += [neighbour(0, 0, 1), neighbour(0, 0, 2), neighbour(0, 0, 3)]
    peers += [sibling, partner]
    for peer in peers:
        pl.semaphore_signal(bar, inc=1, device_id=peer, device_id_type=MESH)

    for load in loads[:5]:
        load.wait()
    for h in range(2):
        rows = pl.ds(h * 256, 256)
        g = gate_v[rows, :].astype(F32)
        u = up_v[rows, :].astype(F32)
        sig = 1.0 / (1.0 + jnp.exp(-g))
        silu = g * sig
        hid[rows, :] = (silu * u).astype(BF16)
        f1[rows, :] = silu
        f2[rows, :] = u * sig * (1.0 + g * (1.0 - sig))
        p_src[h, 0:16, :] = lax.dot_general(am_v[...], hid[rows, :], NT, preferred_element_type=F32)
        p_src[h, 16:32, :] = lax.dot_general(om_v[...], og_v[rows, :], NT, preferred_element_type=F32)
    acc[...] = jnp.zeros_like(acc)

    pl.semaphore_wait(bar, len(peers))

    def remote(src, dst, s_sem, r_sem, dev):
        return pltpu.make_async_remote_copy(
            src_ref=src, dst_ref=dst, send_sem=s_sem, recv_sem=r_sem, device_id=dev, device_id_type=MESH
        )

    def small(src, dst, i, dev):
        return remote(src, dst, small_ssem.at[i], small_rsem.at[i], dev)

    def own_rows(h):
        return og_v.at[pl.ds(pl.multiple_of(h * 256, 256), 256)]

    small(p_src.at[o], p_dst, 0, sibling).start()
    sib_own_c = remote(own_rows(c), buf.at[c, me, c], sib_ssem, own_rsem.at[0], sibling)
    sib_own_o = remote(own_rows(o), buf.at[o, me_other, c], sib_ssem, own_rsem.at[1], sibling)
    sib_own_o.start()
    hops = ((1, 0, 0), (3, 0, 0), (0, 1, 0), (0, 3, 0), (0, 0, 1), (0, 0, 3))

    def send_own(src, k):
        for da, dz, db in hops:
            remote(
                src, buf.at[c, me, k], ssem, rsem.at[irel(-da, -dz, -db) * 2 + k], neighbour(da, dz, db)
            ).start()

    send_own(own_rows(c), c)
    sib_own_c.start()
    local = [
        pltpu.make_async_copy(own_rows(c), buf.at[c, me, c], local_sem.at[0]),
        pltpu.make_async_copy(own_rows(o), buf.at[o, me_other, c], local_sem.at[1]),
    ]
    for copy in local:
        copy.start()
    remote(own_rows(o), buf.at[c, me, o], sib_ssem, own_rsem.at[1], sibling).wait_recv()
    send_own(buf.at[c, me, o], o)

    def wait_half(s, r, k):
        remote(buf.at[c, s, k], buf.at[c, s, k], ssem, rsem.at[r * 2 + k], sibling).wait_recv()

    def wait_whole(s, r):
        remote(buf.at[c, s], buf.at[c, s], ssem, rsem.at[r * 2], sibling).wait_recv()

    def wait_piece(s, r, split):
        @pl.when(split)
        def _():
            wait_half(s, r, 0)
            wait_half(s, r, 1)

        @pl.when(jnp.logical_not(split))
        def _():
            wait_whole(s, r)

    def send_whole(s, r, dev):
        remote(buf.at[c, s], buf.at[c, s], ssem, rsem.at[r * 2], dev).start()

    def send_half(s, k, r, dev):
        remote(buf.at[c, s, k], buf.at[c, s, k], ssem, rsem.at[r * 2 + k], dev).start()

    def send_sib(s, r):
        remote(buf.at[c, s], buf.at[c, s], sib_ssem, sib_rsem.at[r], sibling).start()

    b_up, b_down = neighbour(0, 0, 1), neighbour(0, 0, 3)
    z_up, z_down = neighbour(0, 1, 0), neighbour(0, 3, 0)
    a_up, a_down = neighbour(1, 0, 0), neighbour(3, 0, 0)

    def send_b(da, dz, s):
        send_whole(s, rel(da, dz, 3), b_up)
        send_whole(s, rel(da, dz, 1), b_down)

    def send_z(da, s):
        send_whole(s, rel(da, 3, 0), z_up)
        send_whole(s, rel(da, 1, 0), z_down)

    def place(s):
        mid = lax.rem(lax.div(s + 4, 8), 2)
        q = (1 - mid) * lax.rem(s, 4) + mid * lax.div(lax.rem(s + 4, 8), 2)
        dz = mid * (1 + 2 * lax.rem(s, 2)) + (1 - mid) * 2 * lax.div(s, 12)
        da = q + lax.div(q, 2) * (5 - 2 * q)
        return q, da, dz

    def plane(s):
        q, da, dz = place(s)
        p, r = slot(da, dz, 0), rel(da, dz, 0)

        @pl.when(s == 1)
        def _():
            wait_half(p, r, 0)
            wait_half(p, r, 1)
            send_half(p, 0, irel(2, 0, 0), a_down)

        @pl.when(s == 2)
        def _():
            wait_half(p, r, 0)
            wait_half(p, r, 1)
            send_half(p, 1, irel(2, 0, 0), a_up)

        @pl.when(s == 3)
        def _():
            wait_half(p, r, 0)
            wait_half(p, r, 1)

        @pl.when(s < 4)
        def _():
            send_z(da, p)

        @pl.when(jnp.logical_and(s >= 4, s < 12))
        def _():
            wait_piece(p, r, q == 0)

            @pl.when(dz == 1)
            def _():
                send_half(p, 0, rel(da, 2, 0), z_down)

            @pl.when(dz == 3)
            def _():
                send_half(p, 1, rel(da, 2, 0), z_up)

        @pl.when(s >= 12)
        def _():
            wait_half(p, r, 0)
            wait_half(p, r, 1)

        send_b(da, dz, p)
        send_sib(p, r)

    def cross1(s):
        _, da, dz = place(s)
        for db, k, dev in ((1, 0, b_down), (3, 1, b_up)):
            p, r = slot(da, dz, db), rel(da, dz, db)
            wait_piece(p, r, s == 0)
            send_half(p, k, rel(da, dz, 2), dev)
            send_sib(p, r)

    def cross2(s):
        _, da, dz = place(s)
        p, r = slot(da, dz, 2), rel(da, dz, 2)
        wait_half(p, r, 0)
        wait_half(p, r, 1)
        send_sib(p, r)

    def multiply(h, da, dz, pa, pb_is_row):
        pz = lax.rem(z + dz, 4)
        first = pz * 16 + pa * 4
        total = None
        for i in range(4):
            lhs = jnp.concatenate([buf[h, first + i, 0], buf[h, first + i, 1]], axis=1)
            j = pz * 16 + (1 - h) * (i * 4 + pa) + h * (pa * 4 + i)
            part = lax.dot_general(lhs, w[j], NT, preferred_element_type=F32)
            total = part if total is None else total + part
        acc[h] += total

    def multiply_own(s):
        _, da, dz = place(s)

        @pl.when(s == 0)
        def _():
            local[0].wait()

        multiply(c, da, dz, lax.rem(a + da, 4), None)

    def multiply_sib(s):
        _, da, dz = place(s)
        pa = lax.rem(b + da, 4)
        pz = lax.rem(z + dz, 4)

        def wait_sib(db):
            t = pz * 16 + pa * 4 + lax.rem(a + db, 4)
            remote(buf.at[o, t], buf.at[o, t], sib_ssem, sib_rsem.at[rel(da, dz, db)], sibling).wait_recv()

        @pl.when(s == 0)
        def _():
            local[1].wait()
            remote(own_rows(o), buf.at[o, me_other, o], sib_ssem, own_rsem.at[0], sibling).wait_recv()

        @pl.when(s > 0)
        def _():
            wait_sib(0)

        for db in (1, 3, 2):
            wait_sib(db)
        multiply(o, da, dz, pa, None)

    def dequantize(ch):
        code_load(ch).wait()

        @pl.loop(0, 4)
        def _(i):
            for g in range(2):
                rows = pl.ds(g * 128, 128)
                word = cbuf[ch, rows, pl.ds(pl.multiple_of(i * 256, 256), 256)]
                j = ch * 4 + i
                for part, level in ((0, word), (1, lax.shift_right_logical(word, 4))):
                    col = pl.ds(pl.multiple_of((j + 32 * part) * 256, 256), 256)
                    level = jnp.bitwise_and(level, 15)
                    value = sc_v[g : g + 1, col] * (level - ze_v[g : g + 1, col]).astype(F32)
                    w[j + 32 * part, rows, :] = value.astype(BF16)

    def along_x(d):
        return chip(lax.rem(x + d, 4), y, z, c)

    def along_y(d):
        return chip(x, lax.rem(y + d, 4), z, c)

    def along_z(d):
        return chip(x, y, lax.rem(z + d, 4), c)

    def all_to_all(src, dst, base, way):
        return [small(src(d), dst, base + d - 1, way(d)) for d in (1, 2, 3)]

    def scatter_x():
        return all_to_all(lambda d: r0.at[lax.rem(x + d, 4)], s1.at[x], 1, along_x)

    def sum_z():
        return all_to_all(lambda d: s2.at[z], s2.at[z], 4, along_z)

    def sum_y():
        return all_to_all(lambda d: s3.at[y], s3.at[y], 7, along_y)

    def gather_x():
        return all_to_all(lambda d: s4.at[x], s4.at[x], 10, along_x)

    def share():
        return small(fin.at[c], fin.at[c], 13, sibling)

    def swap():
        return small(ad_mine, ad_peer, 14, partner)

    def begin(copies):
        for copy in copies:
            copy.start()

    def end(copies):
        for copy in copies:
            copy.wait_recv()

    def four(ref):
        return ((ref[0] + ref[1]) + ref[2]) + ref[3]

    def stage1():
        small(p_src.at[o], p_dst, 0, sibling).wait_recv()
        for i in range(4):
            rows = pl.ds(i * 8, 8)
            r0[i] = p_src[c, rows, :] + p_dst[rows, :]
        s1[x] = r0[x]
        begin(scatter_x())

    def stage2():
        end(scatter_x())
        s2[z] = four(s1)
        begin(sum_z())

    def stage3():
        end(sum_z())
        s3[y] = four(s2)
        begin(sum_y())

    def stage4():
        end(sum_y())
        s4[x] = four(s3)
        begin(gather_x())

    def stage5():
        end(gather_x())
        for i in range(4):
            fin[c, pl.ds(i * 8, 8), :] = s4[i]
        share().start()

    def stage6():
        share().wait_recv()
        ain = None
        aout = None
        for h in range(2):
            rows = pl.ds(h * 256, 256)
            left = fin[h, 0:16, :].astype(BF16)
            right = fin[h, 16:32, :].astype(BF16)
            acc[h] += SCALE * lax.dot_general(right, am_v[...], TN, preferred_element_type=F32)
            p1 = jnp.dot(right, hid[rows, :], preferred_element_type=F32)
            p2 = jnp.dot(left, og_v[rows, :], preferred_element_type=F32)
            ain = p1 if ain is None else ain + p1
            aout = p2 if aout is None else aout + p2
        ad_mine[:, 0:256] = (SCALE / tokens) * ain
        ad_mine[:, 256:384] = (SCALE / tokens) * aout
        swap().start()

    def stage7():
        swap().wait_recv()
        ad_sum[...] = ad_mine[...] + ad_peer[...]
        for copy in adapter_out:
            copy.start()

    adapter_out = [
        pltpu.make_async_copy(ad_sum.at[:, 0:256], ain_out, out_sem.at[4]),
        pltpu.make_async_copy(ad_sum.at[:, 256:384], aout_out, out_sem.at[5]),
    ]

    loads[5].wait()
    loads[6].wait()

    @pl.loop(1, STEPS + LAG_SIB)
    def _(s):
        for at, stage in ((1, stage1), (2, stage2), (4, stage3), (6, stage4), (8, stage5), (10, stage6), (13, stage7)):
            pl.when(s == at)(stage)

        @pl.when(s < STEPS)
        def _():
            plane(s)

        @pl.when(jnp.logical_and(s >= LAG1, s < STEPS + LAG1))
        def _():
            cross1(s - LAG1)

        @pl.when(jnp.logical_and(s >= LAG2, s < STEPS + LAG2))
        def _():
            cross2(s - LAG2)

        @pl.when(s <= 4)
        def _():
            dequantize(s * 2 - 2)
            dequantize(s * 2 - 1)

        @pl.when(jnp.logical_and(s >= LAG_OWN, s < STEPS + LAG_OWN))
        def _():
            multiply_own(s - LAG_OWN)

        @pl.when(s >= LAG_SIB)
        def _():
            multiply_sib(s - LAG_SIB)

    outs = []
    for h in range(2):
        rows = pl.ds(h * 256, 256)
        gh = acc[h]
        gres[rows, :] = (gh * f2[rows, :]).astype(BF16)
        ures[rows, :] = (gh * f1[rows, :]).astype(BF16)
        for i, (v, ref) in enumerate(((gres, gate_out), (ures, up_out))):
            copy = pltpu.make_async_copy(v.at[rows], ref.at[rows], out_sem.at[h * 2 + i])
            copy.start()
            outs.append(copy)

    small(p_src.at[o], p_dst, 0, sibling).wait_send()
    for copies in (scatter_x(), sum_z(), sum_y(), gather_x(), [share()], [swap()]):
        for copy in copies:
            copy.wait_send()
    remote(buf.at[0, 0:63], buf.at[0, 0:63], ssem, rsem.at[0], sibling).wait_send()
    remote(buf.at[0], buf.at[0], sib_ssem, rsem.at[0], sibling).wait_send()
    for copy in outs + adapter_out:
        copy.wait()


def local(og, gate, up, codes, scales, zeros, amap, omap):
    rows, cols = og.shape
    hidden = gate.shape[1]
    tokens = rows * lax.axis_size("dp")
    anywhere = pl.BlockSpec(memory_space=pl.ANY)
    dma = pltpu.SemaphoreType.DMA
    return pl.pallas_call(
        functools.partial(kernel, tokens),
        out_shape=(
            jax.ShapeDtypeStruct((rows, hidden), BF16),
            jax.ShapeDtypeStruct((rows, hidden), BF16),
            jax.ShapeDtypeStruct((16, hidden), F32),
            jax.ShapeDtypeStruct((16, cols), F32),
        ),
        in_specs=[anywhere] * 8,
        out_specs=[anywhere] * 4,
        scratch_shapes=[
            pltpu.VMEM((2, 64, 2, 256, 128), BF16),
            pltpu.VMEM((64, 256, 256), BF16),
            pltpu.VMEM((8, 256, 1024), jnp.int32),
            pltpu.VMEM((2, 16384), F32),
            pltpu.VMEM((2, 16384), jnp.int32),
            pltpu.VMEM((512, 256), BF16),
            pltpu.VMEM((512, 256), BF16),
            pltpu.VMEM((16, 256), BF16),
            pltpu.VMEM((16, 128), BF16),
            pltpu.VMEM((512, 128), BF16),
            pltpu.VMEM((512, 256), BF16),
            pltpu.VMEM((512, 256), F32),
            pltpu.VMEM((512, 256), F32),
            pltpu.VMEM((2, 256, 256), F32),
            pltpu.VMEM((512, 256), BF16),
            pltpu.VMEM((512, 256), BF16),
            pltpu.VMEM((2, 32, 256), F32),
            pltpu.VMEM((32, 256), F32),
            pltpu.VMEM((4, 8, 256), F32),
            pltpu.VMEM((4, 8, 256), F32),
            pltpu.VMEM((4, 8, 256), F32),
            pltpu.VMEM((4, 8, 256), F32),
            pltpu.VMEM((4, 8, 256), F32),
            pltpu.VMEM((2, 32, 256), F32),
            pltpu.VMEM((16, 384), F32),
            pltpu.VMEM((16, 384), F32),
            pltpu.VMEM((16, 384), F32),
            dma((7,)),
            dma((8,)),
            dma((2,)),
            dma,
            dma,
            dma((128,)),
            dma((64,)),
            dma((2,)),
            dma((15,)),
            dma((15,)),
            dma((6,)),
        ],
        compiler_params=pltpu.CompilerParams(
            collective_id=0, has_side_effects=True, vmem_limit_bytes=58 * 2**20
        ),
        name="backward",
    )(og, gate, up, codes, scales, zeros, amap, omap)


def solution(mesh):
    in_specs = (
        P("dp", "fsdp"),
        P("dp", "fsdp"),
        P("dp", "fsdp"),
        P("fsdp", None),
        P("fsdp", None),
        P("fsdp", None),
        P(None, "fsdp"),
        P(None, "fsdp"),
    )
    out_specs = (P("dp", "fsdp"), P("dp", "fsdp"), P(None, "fsdp"), P(None, "fsdp"))
    return jax.shard_map(local, mesh=mesh, in_specs=in_specs, out_specs=out_specs, check_vma=False)
```

time: 773 us -> 73.5 us (0.10); the launches traced: 764 us -> 73.3 us
  blocking collectives: 712 us -> 0 us
  Pallas kernels: 0 us -> 66.7 us
  other arithmetic: 21.7 us -> 0 us
  between operations: 14.1 us -> 0.64 us
  matrix products: 11.7 us -> 0 us
    psum x2 -> x0, blocking collectives: 712 us -> none  [the longest x1 706 us: local(): left_full, right_full = lax.psum((left_portion, right_portion), 'fsdp')]
    pallas_call x0 -> x1, Pallas kernels: none -> 66.7 us  [local(): pl.pallas_call(functools.partial(kernel, tokens), out_shape=(jax.ShapeDty...]
    and x1 -> x0, other arithmetic: 11.8 us -> none  [dequantize(): lower = jnp.bitwise_and(codes, 15)]
    dot_general x6 -> x0, matrix products: 11.7 us -> none  [the longest x1 10.5 us: local(): lax.dot_general(lax.all_gather(output_gradient, 'fsdp', axis=1, tiled=Tru...]
    convert_element_type x2 -> x0, other arithmetic: 9.88 us -> none  [the longest x1 9.69 us: dequantize(): return values.reshape(rows, 2 * half).astype(jnp.bfloat16)]
  transfers between devices with their start and end apart: 1 -> 0, of which waited for: 0 -> 0; matrix products, arithmetic and copies ran while one was open for 3% -> 0% of each run, Pallas kernels for 0% -> 0%
where the time goes in v1:
time: 73.5 us; the launch traced here: 73.3 us
  Pallas kernels  66.7 us (91%)
  local copies, waits for them, and re-layouts  5.96 us (8%)
    pallas_call x1, Pallas kernels, local(): pl.pallas_call(functools.partial(kernel, tokens), out_shape=(jax.ShapeDty...  66.7 us
    unnamed x4, local copies, waits for them, and re-layouts  5.96 us

profile of v1, /device:TPU:1, one launch (start us, length us, event | category | flops | bytes accessed | tf_op | source)
XLA Modules:
  0.0 73.3 jit_solution(5068168382374536982)
XLA Ops:
  0.6 66.7 %backward.1 = (bf16[512,256]{1,0:T(8,128)(2,1)}, bf16[512,256]{1,0:T(8,128)(2,1)}, f32[16,256]{1,0:T(8,128)}, f32[16,128]{1,0:T(8,128)}) custom-call(bf16[512,128]{1,0:T(8,128)(2,1)} %og.1, bf16[512,256]{1,0:T(8,128)(2,1)} %gate.1, bf16[512,256]{1,0:T(8,128)(2,1)} %up.1, s32[256,8192]{1,0:T(8,128)} %codes.1, f32[2,16384]{1,0:T(2,128)} %scales.1, ...), custom_call_target="tpu_custom_call" | custom-call | tf_op jit(solution)/shard_map/backward/pallas_call | solution.py:456
  67.3 1.7 %copy.16 = bf16[512,256]{1,0:T(8,128)(2,1)} copy(bf16[512,256]{1,0:T(8,128)(2,1)} %get-tuple-element.8) | data formatting | bytes 524288
  69.0 1.7 %copy.17 = bf16[512,256]{1,0:T(8,128)(2,1)} copy(bf16[512,256]{1,0:T(8,128)(2,1)} %get-tuple-element.9) | data formatting | bytes 524288
  70.7 1.3 %copy.18 = f32[16,256]{1,0:T(8,128)} copy(f32[16,256]{1,0:T(8,128)} %get-tuple-element.10) | data formatting | bytes 32768
  72.0 1.3 %copy.19 = f32[16,128]{1,0:T(8,128)} copy(f32[16,128]{1,0:T(8,128)} %get-tuple-element.11) | data formatting | bytes 16384

commit v2 on v1

v2 whole, which is shorter than its diff:
```python
import functools

import jax
import jax.numpy as jnp
from jax import lax
from jax.experimental import pallas as pl
from jax.experimental.pallas import tpu as pltpu
from jax.sharding import PartitionSpec as P

MESH = pl.DeviceIdType.MESH
F32 = jnp.float32
BF16 = jnp.bfloat16
SCALE = 2.0
LAG1, LAG2, LAG_OWN, LAG_SIB = 3, 6, 7, 8
STEPS = 16
ORDER = ((0, 0), (1, 0), (3, 0), (0, 1), (0, 3), (2, 0), (0, 2), (1, 1), (1, 3), (1, 2), (3, 2), (3, 1), (3, 3), (2, 2), (2, 1), (2, 3))
Z_SENDS = ((2, 1), (6, 3), (8, 2))
Z_HALVES = 2
CROSS_FIRST = (3, 7)
EARLY = 6
STAGES = ((2, 2), (5, 3), (7, 4), (9, 5), (11, 6), (14, 7))
NT = (((1,), (1,)), ((), ()))
TN = (((0,), (0,)), ((), ()))


def kernel(
    tokens,
    og, gate, up, codes, scales, zeros, amap, omap,
    gate_out, up_out, ain_out, aout_out,
    buf, w, cbuf, sc_v, ze_v, gate_v, up_v, am_v, om_v, og_v,
    hid, f1, f2, acc,
    p_src, p_dst, r0, s1, s2, s3, s4, fin, ad_mine, ad_peer,
    load_sem, code_sem, local_sem, ssem, sib_ssem, plane_sem, half_sem, near_sem, far_sem, sib_rsem, own_rsem,
    small_ssem, small_rsem,
):
    dp = lax.axis_index("dp")
    f = lax.axis_index("fsdp")
    c = lax.rem(f, 2)
    y = lax.rem(lax.div(f, 2), 4)
    x = lax.rem(lax.div(f, 8), 4)
    z = lax.div(f, 32)
    a = y + c * (x - y)
    b = x + c * (y - x)
    o = 1 - c

    def chip(px, py, pz, core):
        return (dp, ((pz * 4 + px) * 4 + py) * 2 + core)

    def neighbour(da, dz, db):
        pa, pz, pb = lax.rem(a + da, 4), lax.rem(z + dz, 4), lax.rem(b + db, 4)
        return chip(pb + c * (pa - pb), pa + c * (pb - pa), pz, c)

    sibling = (dp, f + 1 - 2 * c)
    partner = (1 - dp, f)

    def slot(da, dz, db):
        return lax.rem(z + dz, 4) * 16 + lax.rem(a + da, 4) * 4 + lax.rem(b + db, 4)

    def pair(da, dz):
        return lax.rem(dz, 4) * 4 + lax.rem(da, 4)

    me = slot(0, 0, 0)
    me_other = z * 16 + b * 4 + a

    bar = pltpu.get_barrier_semaphore()
    peers = [neighbour(1, 0, 0), neighbour(2, 0, 0), neighbour(3, 0, 0)]
    peers += [neighbour(0, 1, 0), neighbour(0, 2, 0), neighbour(0, 3, 0)]
    peers += [neighbour(0, 0, 1), neighbour(0, 0, 2), neighbour(0, 0, 3)]
    peers += [sibling, partner]
    for peer in peers:
        pl.semaphore_signal(bar, inc=1, device_id=peer, device_id_type=MESH)

    sems = (0, 0, 0, 1, 2, 3, 3)
    pairs = ((og, og_v), (gate, gate_v), (up, up_v), (amap, am_v), (omap, om_v), (scales, sc_v), (zeros, ze_v))
    loads = [pltpu.make_async_copy(p[0], p[1], load_sem.at[i]) for i, p in zip(sems, pairs)]
    for load in loads:
        load.start()

    def code_load(ch):
        return pltpu.make_async_copy(
            codes.at[:, pl.ds(pl.multiple_of(ch * 1024, 1024), 1024)], cbuf.at[ch], code_sem.at[ch // 4]
        )

    for ch in range(8):
        code_load(ch).start()

    def remote(src, dst, s_sem, r_sem, dev):
        return pltpu.make_async_remote_copy(
            src_ref=src, dst_ref=dst, send_sem=s_sem, recv_sem=r_sem, device_id=dev, device_id_type=MESH
        )

    def small(src, dst, i, dev):
        return remote(src, dst, small_ssem, small_rsem.at[i], dev)

    def own_rows(h):
        return og.at[pl.ds(pl.multiple_of(h * 256, 256), 256)]

    a_up, a_down = neighbour(1, 0, 0), neighbour(3, 0, 0)
    b_up, b_down = neighbour(0, 0, 1), neighbour(0, 0, 3)
    z_up, z_down = neighbour(0, 1, 0), neighbour(0, 3, 0)

    def send_own(src, k):
        for i, dev in ((3, z_up), (2, z_down), (1, a_up), (0, a_down)):
            remote(src, buf.at[c, me, k], ssem, half_sem.at[i * 2 + k], dev).start()

    pl.semaphore_wait(bar, len(peers))

    def wait_slots(n, sem):
        remote(buf.at[c, 0:n], buf.at[c, 0:n], ssem, sem, sibling).wait_recv()

    def wait_half(i, k):
        remote(buf.at[c, 0, k], buf.at[c, 0, k], ssem, half_sem.at[i * 2 + k], sibling).wait_recv()

    def send_whole(s, sem, dev):
        remote(buf.at[c, s], buf.at[c, s], ssem, sem, dev).start()

    def send_half(s, k, sem, dev):
        remote(buf.at[c, s, k], buf.at[c, s, k], ssem, sem, dev).start()

    def send_sib(s, da, dz):
        remote(buf.at[c, s], buf.at[c, s], sib_ssem, sib_rsem.at[pair(da, dz)], sibling).start()

    def send_b(da, dz, s):
        send_whole(s, near_sem.at[pair(da, dz)], b_up)
        send_whole(s, near_sem.at[pair(da, dz)], b_down)

    def send_z(da, s):
        send_whole(s, plane_sem.at[pair(da, 3)], z_up)
        send_whole(s, plane_sem.at[pair(da, 1)], z_down)

    def send_a(dz, s):
        send_whole(s, plane_sem.at[pair(3, dz)], a_up)
        send_whole(s, plane_sem.at[pair(1, dz)], a_down)

    sib_own_c = remote(own_rows(c), buf.at[c, me, c], sib_ssem, own_rsem.at[0], sibling)
    sib_own_o = remote(own_rows(o), buf.at[o, me_other, c], sib_ssem, own_rsem.at[1], sibling)
    sib_own_o.start()
    send_own(own_rows(c), c)
    local = [
        pltpu.make_async_copy(own_rows(c), buf.at[c, me, c], local_sem.at[0]),
        pltpu.make_async_copy(own_rows(o), buf.at[o, me_other, c], local_sem.at[1]),
    ]
    for copy in local:
        copy.start()
    sib_own_c.start()

    def partial_sums(h):
        rows = pl.ds(pl.multiple_of(h * 256, 256), 256)
        g = gate_v[rows, :].astype(F32)
        u = up_v[rows, :].astype(F32)
        sig = 1.0 / (1.0 + jnp.exp(-g))
        silu = g * sig
        hid[rows, :] = (silu * u).astype(BF16)
        f1[rows, :] = silu
        f2[rows, :] = u * sig * (1.0 + g * (1.0 - sig))
        p_src[h, 0:16, :] = lax.dot_general(am_v[...], hid[rows, :], NT, preferred_element_type=F32)
        p_src[h, 16:32, :] = lax.dot_general(om_v[...], og_v[rows, :], NT, preferred_element_type=F32)

    pltpu.make_async_copy(w.at[0:5], w.at[0:5], load_sem.at[0]).wait()
    loads[3].wait()
    loads[4].wait()
    partial_sums(o)
    small(p_src.at[o], p_dst, 0, sibling).start()
    remote(own_rows(o), buf.at[c, me, o], sib_ssem, own_rsem.at[1], sibling).wait_recv()
    send_own(buf.at[c, me, o], o)
    local[0].wait()
    send_b(0, 0, me)

    def place(s):
        da = sum(jnp.where(s == i, v[0], 0) for i, v in enumerate(ORDER) if v[0])
        dz = sum(jnp.where(s == i, v[1], 0) for i, v in enumerate(ORDER) if v[1])
        return da, dz

    def plane(s):
        da, dz = place(s)
        p = slot(da, dz, 0)
        along_a = lax.rem(dz, 2) == 0
        one, three = da == 1, da == 3
        own_a = jnp.logical_and(lax.rem(da, 2) == 1, dz == 0)
        own_z = jnp.logical_and(da == 0, lax.rem(dz, 2) == 1)

        @pl.when(jnp.logical_not(jnp.logical_or(own_a, own_z)))
        def _():
            wait_slots(1, plane_sem.at[pair(da, dz)])

        @pl.when(own_a)
        def _():
            pl.when(one)(lambda: wait_half(0, 0))
            pl.when(three)(lambda: wait_half(1, 1))

        @pl.when(along_a)
        def _():
            pl.when(one)(lambda: send_half(p, 0, plane_sem.at[pair(2, dz)], a_down))
            pl.when(three)(lambda: send_half(p, 1, plane_sem.at[pair(2, dz)], a_up))

        @pl.when(own_a)
        def _():
            pl.when(one)(lambda: wait_half(0, 1))
            pl.when(three)(lambda: wait_half(1, 0))

        @pl.when(own_z)
        def _():
            pl.when(dz == 1)(lambda: wait_half(2, 1))
            pl.when(dz == 3)(lambda: wait_half(3, 0))

        @pl.when(jnp.logical_and(da == 0, dz == 2))
        def _():
            send_a(dz, p)

        send_b(da, dz, p)
        send_sib(p, da, dz)

    def z_sends(s):
        @pl.when(s == Z_HALVES)
        def _():
            wait_half(2, 0)
            send_half(slot(0, 1, 0), 0, plane_sem.at[pair(0, 2)], z_down)
            wait_half(3, 1)
            send_half(slot(0, 3, 0), 1, plane_sem.at[pair(0, 2)], z_up)

        for at, which in Z_SENDS:

            @pl.when(s == at)
            def _(which=which):
                send_z(which, slot(which, 0, 0))

    def cross1(s):
        da, dz = place(s)
        wait_slots(2, near_sem.at[pair(da, dz)])
        for db, k, dev in ((1, 0, b_down), (3, 1, b_up)):
            p = slot(da, dz, db)
            send_half(p, k, far_sem.at[pair(da, dz)], dev)
            send_sib(p, da, dz)

    def cross2(s):
        da, dz = place(s)
        wait_slots(1, far_sem.at[pair(da, dz)])
        send_sib(slot(da, dz, 2), da, dz)

    def multiply(h, dz, pa):
        pz = lax.rem(z + dz, 4)
        first = pz * 16 + pa * 4
        total = None
        for i in range(4):
            lhs = jnp.concatenate([buf[h, first + i, 0], buf[h, first + i, 1]], axis=1)
            j = pz * 16 + (1 - h) * (i * 4 + pa) + h * (pa * 4 + i)
            part = lax.dot_general(lhs, w[j], NT, preferred_element_type=F32)
            total = part if total is None else total + part
        acc[h] += total

    def multiply_own(s):
        da, dz = place(s)

        multiply(c, dz, lax.rem(a + da, 4))

    def multiply_sib(s):
        da, dz = place(s)
        pa = lax.rem(b + da, 4)

        def wait_sib(n):
            slots = buf.at[o, 0:n]
            remote(slots, slots, sib_ssem, sib_rsem.at[pair(da, dz)], sibling).wait_recv()

        @pl.when(s == 0)
        def _():
            local[1].wait()
            remote(own_rows(o), buf.at[o, me_other, o], sib_ssem, own_rsem.at[0], sibling).wait_recv()
            wait_sib(3)

        @pl.when(s > 0)
        def _():
            wait_sib(4)

        multiply(o, dz, pa)

    def dequantize(ch):
        @pl.when(ch % 4 == 0)
        def _():
            pltpu.make_async_copy(cbuf.at[0:4], cbuf.at[0:4], code_sem.at[ch // 4]).wait()

        @pl.loop(0, 4)
        def _(i):
            for g in range(2):
                rows = pl.ds(g * 128, 128)
                word = cbuf[ch, rows, pl.ds(pl.multiple_of(i * 256, 256), 256)]
                j = ch * 4 + i
                for part, level in ((0, word), (1, lax.shift_right_logical(word, 4))):
                    col = pl.ds(pl.multiple_of((j + 32 * part) * 256, 256), 256)
                    level = jnp.bitwise_and(level, 15)
                    value = sc_v[g : g + 1, col] * (level - ze_v[g : g + 1, col]).astype(F32)
                    w[j + 32 * part, rows, :] = value.astype(BF16)

    def along_x(d):
        return chip(lax.rem(x + d, 4), y, z, c)

    def along_y(d):
        return chip(x, lax.rem(y + d, 4), z, c)

    def along_z(d):
        return chip(x, y, lax.rem(z + d, 4), c)

    def all_to_all(src, dst, base, way):
        return [small(src(d), dst, base, way(d)) for d in (1, 2, 3)]

    def scatter_x():
        return all_to_all(lambda d: r0.at[lax.rem(x + d, 4)], s1.at[x], 1, along_x)

    def sum_z():
        return all_to_all(lambda d: s2.at[z], s2.at[z], 2, along_z)

    def sum_y():
        return all_to_all(lambda d: s3.at[y], s3.at[y], 3, along_y)

    def gather_x():
        return all_to_all(lambda d: s4.at[x], s4.at[x], 4, along_x)

    def share():
        return small(fin.at[c], fin.at[c], 5, sibling)

    def swap():
        return small(ad_mine, ad_peer, 6, partner)

    def begin(copies):
        for copy in copies:
            copy.start()

    def end(ref, i):
        small(ref.at[0:3], ref.at[0:3], i, sibling).wait_recv()

    def four(ref):
        return ((ref[0] + ref[1]) + ref[2]) + ref[3]

    def stage1():
        small(p_src.at[o], p_dst, 0, sibling).wait_recv()
        for i in range(4):
            rows = pl.ds(i * 8, 8)
            r0[i] = p_src[c, rows, :] + p_dst[rows, :]
        s1[x] = r0[x]
        begin(scatter_x())

    def stage2():
        end(s1, 1)
        s2[z] = four(s1)
        begin(sum_z())

    def stage3():
        end(s2, 2)
        s3[y] = four(s2)
        begin(sum_y())

    def stage4():
        end(s3, 3)
        s4[x] = four(s3)
        begin(gather_x())

    def stage5():
        end(s4, 4)
        for i in range(4):
            fin[c, pl.ds(i * 8, 8), :] = s4[i]
        share().start()

    def stage6():
        share().wait_recv()
        ain = None
        aout = None
        for h in range(2):
            rows = pl.ds(h * 256, 256)
            left = fin[h, 0:16, :].astype(BF16)
            right = fin[h, 16:32, :].astype(BF16)
            acc[h] += SCALE * lax.dot_general(right, am_v[...], TN, preferred_element_type=F32)
            p1 = jnp.dot(right, hid[rows, :], preferred_element_type=F32)
            p2 = jnp.dot(left, og_v[rows, :], preferred_element_type=F32)
            ain = p1 if ain is None else ain + p1
            aout = p2 if aout is None else aout + p2
        ad_mine[:, 0:256] = (SCALE / tokens) * ain
        ad_mine[:, 256:384] = (SCALE / tokens) * aout
        swap().start()

    def stage7():
        swap().wait_recv()
        ain_out[...] = ad_mine[:, 0:256] + ad_peer[:, 0:256]
        aout_out[...] = ad_mine[:, 256:384] + ad_peer[:, 256:384]

    partial_sums(c)
    stage1()
    acc[...] = jnp.zeros_like(acc)
    pltpu.make_async_copy(w.at[0:2], w.at[0:2], load_sem.at[3]).wait()
    for ch in range(EARLY):
        dequantize(ch)

    @pl.loop(1, STEPS + LAG_SIB)
    def _(s):
        for at, stage in STAGES:
            pl.when(s == at)((stage2, stage3, stage4, stage5, stage6, stage7)[stage - 2])

        early = jnp.logical_and(s >= CROSS_FIRST[0], s < CROSS_FIRST[1])

        @pl.when(jnp.logical_and(s < STEPS, jnp.logical_not(early)))
        def _():
            plane(s)

        z_sends(s)

        @pl.when(jnp.logical_and(s >= LAG1, s < STEPS + LAG1))
        def _():
            cross1(s - LAG1)

        @pl.when(early)
        def _():
            plane(s)

        @pl.when(s <= 8 - EARLY)
        def _():
            dequantize(s + EARLY - 1)

        @pl.when(jnp.logical_and(s >= LAG_OWN, s < STEPS + LAG_OWN))
        def _():
            multiply_own(s - LAG_OWN)

        @pl.when(s >= LAG_SIB)
        def _():
            multiply_sib(s - LAG_SIB)

        @pl.when(jnp.logical_and(s >= LAG2, s < STEPS + LAG2))
        def _():
            cross2(s - LAG2)

    for h in range(2):
        rows = pl.ds(h * 256, 256)
        gh = acc[h]
        gate_out[rows, :] = (gh * f2[rows, :]).astype(BF16)
        up_out[rows, :] = (gh * f1[rows, :]).astype(BF16)

    remote(f1.at[0:184], f1.at[0:184], small_ssem, own_rsem.at[0], sibling).wait_send()
    remote(buf.at[0, 0:63], buf.at[0, 0:63], ssem, own_rsem.at[0], sibling).wait_send()
    remote(buf.at[0], buf.at[0], sib_ssem, own_rsem.at[0], sibling).wait_send()


def local(og, gate, up, codes, scales, zeros, amap, omap):
    rows, cols = og.shape
    hidden = gate.shape[1]
    tokens = rows * lax.axis_size("dp")
    anywhere = pl.BlockSpec(memory_space=pl.ANY)
    dma = pltpu.SemaphoreType.DMA
    shapes = (
        jax.ShapeDtypeStruct((rows, hidden), BF16),
        jax.ShapeDtypeStruct((rows, hidden), BF16),
        jax.ShapeDtypeStruct((16, hidden), F32),
        jax.ShapeDtypeStruct((16, cols), F32),
    )
    return pl.pallas_call(
        functools.partial(kernel, tokens),
        out_shape=tuple(pltpu.VMEM(v.shape, v.dtype) for v in shapes),
        in_specs=[anywhere] * 8,
        out_specs=[pl.BlockSpec(memory_space=pltpu.VMEM)] * 4,
        scratch_shapes=[
            pltpu.VMEM((2, 64, 2, 256, 128), BF16),
            pltpu.VMEM((64, 256, 256), BF16),
            pltpu.VMEM((8, 256, 1024), jnp.int32),
            pltpu.VMEM((2, 16384), F32),
            pltpu.VMEM((2, 16384), jnp.int32),
            pltpu.VMEM((512, 256), BF16),
            pltpu.VMEM((512, 256), BF16),
            pltpu.VMEM((16, 256), BF16),
            pltpu.VMEM((16, 128), BF16),
            pltpu.VMEM((512, 128), BF16),
            pltpu.VMEM((512, 256), BF16),
            pltpu.VMEM((512, 256), F32),
            pltpu.VMEM((512, 256), F32),
            pltpu.VMEM((2, 256, 256), F32),
            pltpu.VMEM((2, 32, 256), F32),
            pltpu.VMEM((32, 256), F32),
            pltpu.VMEM((4, 8, 256), F32),
            pltpu.VMEM((4, 8, 256), F32),
            pltpu.VMEM((4, 8, 256), F32),
            pltpu.VMEM((4, 8, 256), F32),
            pltpu.VMEM((4, 8, 256), F32),
            pltpu.VMEM((2, 32, 256), F32),
            pltpu.VMEM((16, 384), F32),
            pltpu.VMEM((16, 384), F32),
            dma((4,)),
            dma((2,)),
            dma((2,)),
            dma,
            dma,
            dma((16,)),
            dma((8,)),
            dma((16,)),
            dma((16,)),
            dma((16,)),
            dma((2,)),
            dma,
            dma((7,)),
        ],
        compiler_params=pltpu.CompilerParams(
            collective_id=0, has_side_effects=True, vmem_limit_bytes=58 * 2**20
        ),
        name="backward",
    )(og, gate, up, codes, scales, zeros, amap, omap)


def solution(mesh):
    in_specs = (
        P("dp", "fsdp"),
        P("dp", "fsdp"),
        P("dp", "fsdp"),
        P("fsdp", None),
        P("fsdp", None),
        P("fsdp", None),
        P(None, "fsdp"),
        P(None, "fsdp"),
    )
    out_specs = (P("dp", "fsdp"), P("dp", "fsdp"), P(None, "fsdp"), P(None, "fsdp"))
    return jax.shard_map(local, mesh=mesh, in_specs=in_specs, out_specs=out_specs, check_vma=False)
```

time: 73.5 us -> 63.9 us (0.87)
  Pallas kernels: 66.7 us -> 60.5 us
  local copies, waits for them, and re-layouts: 5.96 us -> 2.61 us
    pallas_call x1, Pallas kernels: 66.7 us -> 60.5 us  [local(): pl.pallas_call(functools.partial(kernel, tokens), out_shape=tuple((pltpu....]
    unnamed x4, local copies, waits for them, and re-layouts: 5.96 us -> 2.61 us
where the time goes in v2:
time: 63.9 us; the launch traced here: 63.7 us
  Pallas kernels  60.5 us (95%)
  local copies, waits for them, and re-layouts  2.61 us (4%)
  between operations  0.64 us (1%)
    pallas_call x1, Pallas kernels, local(): pl.pallas_call(functools.partial(kernel, tokens), out_shape=tuple((pltpu....  60.5 us
    unnamed x4, local copies, waits for them, and re-layouts  2.61 us

profile of v2, /device:TPU:1, one launch (start us, length us, event | category | flops | bytes accessed | tf_op | source)
XLA Modules:
  0.0 63.7 jit_solution(49843250762671357)
XLA Ops:
  0.6 60.5 %backward.1 = (bf16[512,256]{1,0:T(8,128)(2,1)S(1)}, bf16[512,256]{1,0:T(8,128)(2,1)S(1)}, f32[16,256]{1,0:T(8,128)S(1)}, f32[16,128]{1,0:T(8,128)S(1)}) custom-call(bf16[512,128]{1,0:T(8,128)(2,1)} %og.1, bf16[512,256]{1,0:T(8,128)(2,1)} %gate.1, bf16[512,256]{1,0:T(8,128)(2,1)} %up.1, s32[256,8192]{1,0:T(8,128)} %codes.1, f32[2,16384]{1,0:T(2,128)} %scales.1, ...), custom_call_target="tpu_custom_call" | custom-call | tf_op jit(solution)/shard_map/backward/pallas_call | solution.py:451
  61.1 0.7 %copy.16 = bf16[512,256]{1,0:T(8,128)(2,1)} copy(bf16[512,256]{1,0:T(8,128)(2,1)S(1)} %get-tuple-element.4) | data formatting | bytes 524288
  61.8 0.6 copy.19
  62.4 0.6 copy.18
  63.0 0.7 %copy.17 = bf16[512,256]{1,0:T(8,128)(2,1)} copy(bf16[512,256]{1,0:T(8,128)(2,1)S(1)} %get-tuple-element.5) | data formatting | bytes 524288

commit v3 on v2

--- a/solution.py
+++ b/solution.py
@@ -14,11 +14,11 @@
 LAG1, LAG2, LAG_OWN, LAG_SIB = 3, 6, 7, 8
 STEPS = 16
 ORDER = ((0, 0), (1, 0), (3, 0), (0, 1), (0, 3), (2, 0), (0, 2), (1, 1), (1, 3), (1, 2), (3, 2), (3, 1), (3, 3), (2, 2), (2, 1), (2, 3))
-Z_SENDS = ((2, 1), (6, 3), (8, 2))
-Z_HALVES = 2
+Z_SENDS = ((3, 1), (6, 3), (8, 2))
+Z_HALVES = (2, 3)
 CROSS_FIRST = (3, 7)
 EARLY = 6
-STAGES = ((2, 2), (5, 3), (7, 4), (9, 5), (11, 6), (14, 7))
+STAGES = ((4, 1), (6, 2), (9, 3), (11, 4), (13, 5), (14, 6), (17, 7))
 NT = (((1,), (1,)), ((), ()))
 TN = (((0,), (0,)), ((), ()))
 
@@ -46,9 +46,9 @@
     def chip(px, py, pz, core):
         return (dp, ((pz * 4 + px) * 4 + py) * 2 + core)
 
-    def neighbour(da, dz, db):
+    def neighbour(da, dz, db, core=None):
         pa, pz, pb = lax.rem(a + da, 4), lax.rem(z + dz, 4), lax.rem(b + db, 4)
-        return chip(pb + c * (pa - pb), pa + c * (pb - pa), pz, c)
+        return chip(pb + c * (pa - pb), pa + c * (pb - pa), pz, c if core is None else core)
 
     sibling = (dp, f + 1 - 2 * c)
     partner = (1 - dp, f)
@@ -63,9 +63,10 @@
     me_other = z * 16 + b * 4 + a
 
     bar = pltpu.get_barrier_semaphore()
-    peers = [neighbour(1, 0, 0), neighbour(2, 0, 0), neighbour(3, 0, 0)]
-    peers += [neighbour(0, 1, 0), neighbour(0, 2, 0), neighbour(0, 3, 0)]
-    peers += [neighbour(0, 0, 1), neighbour(0, 0, 2), neighbour(0, 0, 3)]
+    peers = [neighbour(1, 0, 0), neighbour(3, 0, 0)]
+    peers += [neighbour(0, 1, 0), neighbour(0, 3, 0)]
+    peers += [neighbour(0, 0, 1), neighbour(0, 0, 3)]
+    peers += [neighbour(1, 0, 0, o), neighbour(3, 0, 0, o)]
     peers += [sibling, partner]
     for peer in peers:
         pl.semaphore_signal(bar, inc=1, device_id=peer, device_id_type=MESH)
@@ -99,8 +100,8 @@
     b_up, b_down = neighbour(0, 0, 1), neighbour(0, 0, 3)
     z_up, z_down = neighbour(0, 1, 0), neighbour(0, 3, 0)
 
-    def send_own(src, k):
-        for i, dev in ((3, z_up), (2, z_down), (1, a_up), (0, a_down)):
+    def send_own_z(src, k):
+        for i, dev in ((3, z_up), (2, z_down)):
             remote(src, buf.at[c, me, k], ssem, half_sem.at[i * 2 + k], dev).start()
 
     pl.semaphore_wait(bar, len(peers))
@@ -135,7 +136,14 @@
     sib_own_c = remote(own_rows(c), buf.at[c, me, c], sib_ssem, own_rsem.at[0], sibling)
     sib_own_o = remote(own_rows(o), buf.at[o, me_other, c], sib_ssem, own_rsem.at[1], sibling)
     sib_own_o.start()
-    send_own(own_rows(c), c)
+    send_own_z(own_rows(c), c)
+    for i, h, place_of, dev in (
+        (1, c, me, a_up),
+        (0, c, me, a_down),
+        (1, o, me_other, neighbour(0, 0, 1, o)),
+        (0, o, me_other, neighbour(0, 0, 3, o)),
+    ):
+        remote(own_rows(h), buf.at[h, place_of, c], ssem, half_sem.at[i * 2 + c], dev).start()
     local = [
         pltpu.make_async_copy(own_rows(c), buf.at[c, me, c], local_sem.at[0]),
         pltpu.make_async_copy(own_rows(o), buf.at[o, me_other, c], local_sem.at[1]),
@@ -162,7 +170,7 @@
     partial_sums(o)
     small(p_src.at[o], p_dst, 0, sibling).start()
     remote(own_rows(o), buf.at[c, me, o], sib_ssem, own_rsem.at[1], sibling).wait_recv()
-    send_own(buf.at[c, me, o], o)
+    send_own_z(buf.at[c, me, o], o)
     local[0].wait()
     send_b(0, 0, me)
 
@@ -200,8 +208,8 @@
 
         @pl.when(own_z)
         def _():
-            pl.when(dz == 1)(lambda: wait_half(2, 1))
-            pl.when(dz == 3)(lambda: wait_half(3, 0))
+            pl.when(dz == 1)(lambda: wait_half(2, o))
+            pl.when(dz == 3)(lambda: wait_half(3, c))
 
         @pl.when(jnp.logical_and(da == 0, dz == 2))
         def _():
@@ -211,12 +219,15 @@
         send_sib(p, da, dz)
 
     def z_sends(s):
-        @pl.when(s == Z_HALVES)
-        def _():
-            wait_half(2, 0)
-            send_half(slot(0, 1, 0), 0, plane_sem.at[pair(0, 2)], z_down)
-            wait_half(3, 1)
-            send_half(slot(0, 3, 0), 1, plane_sem.at[pair(0, 2)], z_up)
+        @pl.when(s == Z_HALVES[0])
+        def _():
+            wait_half(2, c)
+            send_half(slot(0, 1, 0), c, plane_sem.at[pair(0, 2)], z_down)
+
+        @pl.when(s == Z_HALVES[1])
+        def _():
+            wait_half(3, o)
+            send_half(slot(0, 3, 0), o, plane_sem.at[pair(0, 2)], z_up)
 
         for at, which in Z_SENDS:
 
@@ -382,16 +393,17 @@
         aout_out[...] = ad_mine[:, 256:384] + ad_peer[:, 256:384]
 
     partial_sums(c)
-    stage1()
     acc[...] = jnp.zeros_like(acc)
     pltpu.make_async_copy(w.at[0:2], w.at[0:2], load_sem.at[3]).wait()
     for ch in range(EARLY):
         dequantize(ch)
 
+    stages = (stage1, stage2, stage3, stage4, stage5, stage6, stage7)
+
     @pl.loop(1, STEPS + LAG_SIB)
     def _(s):
         for at, stage in STAGES:
-            pl.when(s == at)((stage2, stage3, stage4, stage5, stage6, stage7)[stage - 2])
+            pl.when(s == at)(stages[stage - 1])
 
         early = jnp.logical_and(s >= CROSS_FIRST[0], s < CROSS_FIRST[1])
 
@@ -399,12 +411,12 @@
         def _():
             plane(s)
 
+        @pl.when(jnp.logical_and(s >= LAG1, s < STEPS + LAG1))
+        def _():
+            cross1(s - LAG1)
+
         z_sends(s)
 
-        @pl.when(jnp.logical_and(s >= LAG1, s < STEPS + LAG1))
-        def _():
-            cross1(s - LAG1)
-
         @pl.when(early)
         def _():
             plane(s)
@@ -413,17 +425,17 @@
         def _():
             dequantize(s + EARLY - 1)
 
+        @pl.when(s >= LAG_SIB)
+        def _():
+            multiply_sib(s - LAG_SIB)
+
+        @pl.when(jnp.logical_and(s >= LAG2, s < STEPS + LAG2))
+        def _():
+            cross2(s - LAG2)
+
         @pl.when(jnp.logical_and(s >= LAG_OWN, s < STEPS + LAG_OWN))
         def _():
             multiply_own(s - LAG_OWN)
-
-        @pl.when(s >= LAG_SIB)
-        def _():
-            multiply_sib(s - LAG_SIB)
-
-        @pl.when(jnp.logical_and(s >= LAG2, s < STEPS + LAG2))
-        def _():
-            cross2(s - LAG2)
 
     for h in range(2):
         rows = pl.ds(h * 256, 256)
@@ -434,6 +446,15 @@
     remote(f1.at[0:184], f1.at[0:184], small_ssem, own_rsem.at[0], sibling).wait_send()
     remote(buf.at[0, 0:63], buf.at[0, 0:63], ssem, own_rsem.at[0], sibling).wait_send()
     remote(buf.at[0], buf.at[0], sib_ssem, own_rsem.at[0], sibling).wait_send()
+
+
+def hand_over(*refs):
+    n = len(refs) // 2
+    copies = [pltpu.make_async_copy(refs[i], refs[n + i], refs[-1].at[i]) for i in range(n)]
+    for copy in copies:
+        copy.start()
+    for copy in copies:
+        copy.wait()
 
 
 def local(og, gate, up, codes, scales, zeros, amap, omap):
@@ -448,7 +469,7 @@
         jax.ShapeDtypeStruct((16, hidden), F32),
         jax.ShapeDtypeStruct((16, cols), F32),
     )
-    return pl.pallas_call(
+    results = pl.pallas_call(
         functools.partial(kernel, tokens),
         out_shape=tuple(pltpu.VMEM(v.shape, v.dtype) for v in shapes),
         in_specs=[anywhere] * 8,
@@ -497,6 +518,14 @@
         ),
         name="backward",
     )(og, gate, up, codes, scales, zeros, amap, omap)
+    return pl.pallas_call(
+        hand_over,
+        out_shape=shapes,
+        in_specs=[pl.BlockSpec(memory_space=pltpu.VMEM)] * 4,
+        out_specs=[anywhere] * 4,
+        scratch_shapes=[dma((4,))],
+        name="hand_over",
+    )(*(pltpu.with_memory_space_constraint(v, pltpu.VMEM) for v in results))
 
 
 def solution(mesh):

time: 63.9 us -> 57.4 us (0.90)
  Pallas kernels: 60.5 us -> 56.3 us
  local copies, waits for them, and re-layouts: 2.61 us -> 0 us
    pallas_call x1, Pallas kernels: 60.5 us -> 55.5 us  [local(): pl.pallas_call(functools.partial(kernel, tokens), out_shape=tuple((pltpu....]
    unnamed x4 -> x0, local copies, waits for them, and re-layouts: 2.61 us -> none
    pallas_call x0 -> x1, Pallas kernels: none -> 0.83 us  [local(): pl.pallas_call(hand_over, out_shape=shapes, in_specs=[pl.BlockSpec(memory...]
where the time goes in v3:
time: 57.4 us; the launch traced here: 57 us
  Pallas kernels  56.3 us (98%)
  between operations  0.64 us (1%)
    pallas_call x1, Pallas kernels, local(): pl.pallas_call(functools.partial(kernel, tokens), out_shape=tuple((pltpu....  55.5 us

profile of v3, /device:TPU:1, one launch (start us, length us, event | category | flops | bytes accessed | tf_op | source)
XLA Modules:
  0.0 57.0 jit_solution(13561999490307298373)
XLA Ops:
  0.6 55.5 %backward.1 = (bf16[512,256]{1,0:T(8,128)(2,1)S(1)}, bf16[512,256]{1,0:T(8,128)(2,1)S(1)}, f32[16,256]{1,0:T(8,128)S(1)}, f32[16,128]{1,0:T(8,128)S(1)}) custom-call(bf16[512,128]{1,0:T(8,128)(2,1)} %og.1, bf16[512,256]{1,0:T(8,128)(2,1)} %gate.1, bf16[512,256]{1,0:T(8,128)(2,1)} %up.1, s32[256,8192]{1,0:T(8,128)} %codes.1, f32[2,16384]{1,0:T(2,128)} %scales.1, ...), custom_call_target="tpu_custom_call" | custom-call | tf_op jit(solution)/shard_map/backward/pallas_call | solution.py:472
  56.1 0.8 %hand_over.1 = (bf16[512,256]{1,0:T(8,128)(2,1)}, bf16[512,256]{1,0:T(8,128)(2,1)}, f32[16,256]{1,0:T(8,128)}, f32[16,128]{1,0:T(8,128)}) custom-call(bf16[512,256]{1,0:T(8,128)(2,1)S(1)} %get-tuple-element.8.refs_0_, bf16[512,256]{1,0:T(8,128)(2,1)S(1)} %get-tuple-element.9.refs_1_, f32[16,256]{1,0:T(8,128)S(1)} %get-tuple-element.10.refs_2_, ...), custom_call_target="tpu_custom_call" | custom-call | tf_op jit(solution)/shard_map/hand_over/pallas_call | solution.py:521

commit v4 on v3

--- a/solution.py
+++ b/solution.py
@@ -14,11 +14,13 @@
 LAG1, LAG2, LAG_OWN, LAG_SIB = 3, 6, 7, 8
 STEPS = 16
 ORDER = ((0, 0), (1, 0), (3, 0), (0, 1), (0, 3), (2, 0), (0, 2), (1, 1), (1, 3), (1, 2), (3, 2), (3, 1), (3, 3), (2, 2), (2, 1), (2, 3))
-Z_SENDS = ((3, 1), (6, 3), (8, 2))
+Z_SENDS = ((3, 1), (8, 3), (10, 2))
 Z_HALVES = (2, 3)
-CROSS_FIRST = (3, 7)
+Z_FAR = 12
+SOONER = (13, 14)
+CROSS_FIRST = (3, 9)
 EARLY = 6
-STAGES = ((4, 1), (6, 2), (9, 3), (11, 4), (13, 5), (14, 6), (17, 7))
+STAGES = ((4, 1), (7, 2), (10, 3), (12, 4), (14, 5), (16, 6), (18, 7))
 NT = (((1,), (1,)), ((), ()))
 TN = (((0,), (0,)), ((), ()))
 
@@ -235,12 +237,23 @@
             def _(which=which):
                 send_z(which, slot(which, 0, 0))
 
+        @pl.when(s == Z_FAR)
+        def _():
+            p = slot(2, 0, 2)
+            send_whole(p, far_sem.at[pair(2, 3)], z_up)
+            send_whole(p, far_sem.at[pair(2, 1)], z_down)
+
     def cross1(s):
         da, dz = place(s)
         wait_slots(2, near_sem.at[pair(da, dz)])
+        along_b = jnp.logical_not(jnp.logical_and(da == 2, lax.rem(dz, 2) == 1))
         for db, k, dev in ((1, 0, b_down), (3, 1, b_up)):
             p = slot(da, dz, db)
-            send_half(p, k, far_sem.at[pair(da, dz)], dev)
+
+            @pl.when(along_b)
+            def _(p=p, k=k, dev=dev):
+                send_half(p, k, far_sem.at[pair(da, dz)], dev)
+
             send_sib(p, da, dz)
 
     def cross2(s):
@@ -400,7 +413,11 @@
 
     stages = (stage1, stage2, stage3, stage4, stage5, stage6, stage7)
 
-    @pl.loop(1, STEPS + LAG_SIB)
+    def catch_up(do, s, lag, sooner):
+        late = jnp.where(s < sooner, s - lag, s - lag + 1)
+        lax.fori_loop(jnp.maximum(jnp.where(s <= sooner, s - lag, late), 0), late + 1, lambda i, _: do(i), None)
+
+    @pl.loop(1, STEPS + LAG1)
     def _(s):
         for at, stage in STAGES:
             pl.when(s == at)(stages[stage - 1])
@@ -425,17 +442,24 @@
         def _():
             dequantize(s + EARLY - 1)
 
-        @pl.when(s >= LAG_SIB)
-        def _():
-            multiply_sib(s - LAG_SIB)
-
-        @pl.when(jnp.logical_and(s >= LAG2, s < STEPS + LAG2))
+        catch_up(multiply_sib, s, LAG_SIB, SOONER[1])
+
+        @pl.when(s >= LAG2)
         def _():
             cross2(s - LAG2)
 
-        @pl.when(jnp.logical_and(s >= LAG_OWN, s < STEPS + LAG_OWN))
-        def _():
-            multiply_own(s - LAG_OWN)
+        catch_up(multiply_own, s, LAG_OWN, SOONER[0])
+
+    @pl.loop(STEPS + LAG1 - LAG2, STEPS)
+    def _(s):
+        cross2(s)
+
+    @pl.loop(STEPS + LAG1 - LAG2, STEPS)
+    def _(s):
+        multiply_own(s)
+        multiply_sib(s - 1)
+
+    multiply_sib(STEPS - 1)
 
     for h in range(2):
         rows = pl.ds(h * 256, 256)

time: 57.4 us -> 56.1 us (0.977)
  Pallas kernels: 56.3 us -> 55.3 us
    pallas_call x1, Pallas kernels: 55.5 us -> 54.5 us  [local(): pl.pallas_call(functools.partial(kernel, tokens), out_shape=tuple((pltpu....]
where the time goes in v4:
time: 56.1 us; the launch traced here: 55.9 us
  Pallas kernels  55.3 us (99%)
  between operations  0.64 us (1%)
    pallas_call x1, Pallas kernels, local(): pl.pallas_call(functools.partial(kernel, tokens), out_shape=tuple((pltpu....  54.5 us

profile of v4, /device:TPU:1, one launch (start us, length us, event | category | flops | bytes accessed | tf_op | source)
XLA Modules:
  0.0 55.9 jit_solution(16076278547922566062)
XLA Ops:
  0.6 54.5 %backward.1 = (bf16[512,256]{1,0:T(8,128)(2,1)S(1)}, bf16[512,256]{1,0:T(8,128)(2,1)S(1)}, f32[16,256]{1,0:T(8,128)S(1)}, f32[16,128]{1,0:T(8,128)S(1)}) custom-call(bf16[512,128]{1,0:T(8,128)(2,1)} %og.1, bf16[512,256]{1,0:T(8,128)(2,1)} %gate.1, bf16[512,256]{1,0:T(8,128)(2,1)} %up.1, s32[256,8192]{1,0:T(8,128)} %codes.1, f32[2,16384]{1,0:T(2,128)} %scales.1, ...), custom_call_target="tpu_custom_call" | custom-call | tf_op jit(solution)/shard_map/backward/pallas_call | solution.py:496
  55.1 0.8 %hand_over.1 = (bf16[512,256]{1,0:T(8,128)(2,1)}, bf16[512,256]{1,0:T(8,128)(2,1)}, f32[16,256]{1,0:T(8,128)}, f32[16,128]{1,0:T(8,128)}) custom-call(bf16[512,256]{1,0:T(8,128)(2,1)S(1)} %get-tuple-element.8.refs_0_, bf16[512,256]{1,0:T(8,128)(2,1)S(1)} %get-tuple-element.9.refs_1_, f32[16,256]{1,0:T(8,128)S(1)} %get-tuple-element.10.refs_2_, ...), custom_call_target="tpu_custom_call" | custom-call | tf_op jit(solution)/shard_map/hand_over/pallas_call | solution.py:545

commit v5 on v3

--- a/solution.py
+++ b/solution.py
@@ -14,11 +14,13 @@
 LAG1, LAG2, LAG_OWN, LAG_SIB = 3, 6, 7, 8
 STEPS = 16
 ORDER = ((0, 0), (1, 0), (3, 0), (0, 1), (0, 3), (2, 0), (0, 2), (1, 1), (1, 3), (1, 2), (3, 2), (3, 1), (3, 3), (2, 2), (2, 1), (2, 3))
-Z_SENDS = ((3, 1), (6, 3), (8, 2))
+Z_SENDS = ((3, 1), (8, 3), (10, 2))
 Z_HALVES = (2, 3)
-CROSS_FIRST = (3, 7)
+Z_FAR = ((12, 2),)
+SOONER = (13, 17)
+CROSS_FIRST = (3, 9)
 EARLY = 6
-STAGES = ((4, 1), (6, 2), (9, 3), (11, 4), (13, 5), (14, 6), (17, 7))
+STAGES = ((4, 1), (7, 2), (10, 3), (12, 4), (14, 5), (16, 6))
 NT = (((1,), (1,)), ((), ()))
 TN = (((0,), (0,)), ((), ()))
 
@@ -235,12 +237,26 @@
             def _(which=which):
                 send_z(which, slot(which, 0, 0))
 
+        for at, which in Z_FAR:
+
+            @pl.when(s == at)
+            def _(which=which):
+                p = slot(which, 0, 2)
+                send_whole(p, far_sem.at[pair(which, 3)], z_up)
+                send_whole(p, far_sem.at[pair(which, 1)], z_down)
+
     def cross1(s):
         da, dz = place(s)
         wait_slots(2, near_sem.at[pair(da, dz)])
+        by_z = functools.reduce(jnp.logical_or, [da == which for _, which in Z_FAR])
+        along_b = jnp.logical_not(jnp.logical_and(by_z, lax.rem(dz, 2) == 1))
         for db, k, dev in ((1, 0, b_down), (3, 1, b_up)):
             p = slot(da, dz, db)
-            send_half(p, k, far_sem.at[pair(da, dz)], dev)
+
+            @pl.when(along_b)
+            def _(p=p, k=k, dev=dev):
+                send_half(p, k, far_sem.at[pair(da, dz)], dev)
+
             send_sib(p, da, dz)
 
     def cross2(s):
@@ -251,12 +267,9 @@
     def multiply(h, dz, pa):
         pz = lax.rem(z + dz, 4)
         first = pz * 16 + pa * 4
-        total = None
-        for i in range(4):
-            lhs = jnp.concatenate([buf[h, first + i, 0], buf[h, first + i, 1]], axis=1)
-            j = pz * 16 + (1 - h) * (i * 4 + pa) + h * (pa * 4 + i)
-            part = lax.dot_general(lhs, w[j], NT, preferred_element_type=F32)
-            total = part if total is None else total + part
+        lhs = jnp.concatenate([buf[h, first + i, k] for i in range(4) for k in range(2)], axis=1)
+        rhs = jnp.concatenate([w[pz * 16 + (1 - h) * (i * 4 + pa) + h * (pa * 4 + i)] for i in range(4)], axis=1)
+        total = lax.dot_general(lhs, rhs, NT, preferred_element_type=F32)
         acc[h] += total
 
     def multiply_own(s):
@@ -395,12 +408,16 @@
     partial_sums(c)
     acc[...] = jnp.zeros_like(acc)
     pltpu.make_async_copy(w.at[0:2], w.at[0:2], load_sem.at[3]).wait()
-    for ch in range(EARLY):
-        dequantize(ch)
+    pl.loop(0, EARLY)(dequantize)
 
     stages = (stage1, stage2, stage3, stage4, stage5, stage6, stage7)
 
-    @pl.loop(1, STEPS + LAG_SIB)
+    last = STEPS + LAG1 - 1
+
+    def run(do, first, stop):
+        lax.fori_loop(jnp.maximum(first, 0), stop, lambda i, _: do(i), None)
+
+    @pl.loop(1, last + 2)
     def _(s):
         for at, stage in STAGES:
             pl.when(s == at)(stages[stage - 1])
@@ -425,17 +442,17 @@
         def _():
             dequantize(s + EARLY - 1)
 
-        @pl.when(s >= LAG_SIB)
-        def _():
-            multiply_sib(s - LAG_SIB)
-
-        @pl.when(jnp.logical_and(s >= LAG2, s < STEPS + LAG2))
-        def _():
-            cross2(s - LAG2)
-
-        @pl.when(jnp.logical_and(s >= LAG_OWN, s < STEPS + LAG_OWN))
-        def _():
-            multiply_own(s - LAG_OWN)
+        first = jnp.where(s <= SOONER[1], s - LAG_SIB, s - LAG_SIB + 1)
+        stop = jnp.where(s < SOONER[1], s - LAG_SIB + 1, s - LAG_SIB + 2)
+        run(multiply_sib, first, jnp.where(s > last, STEPS, stop))
+
+        run(cross2, jnp.where(s > last, STEPS, s - LAG2), jnp.where(s < last, s - LAG2 + 1, STEPS))
+
+        first = jnp.where(s <= SOONER[0], s - LAG_OWN, s - LAG_OWN + 1)
+        stop = jnp.where(s < SOONER[0], s - LAG_OWN + 1, s - LAG_OWN + 2)
+        run(multiply_own, jnp.where(s > last, STEPS, first), jnp.where(s < last, stop, STEPS))
+
+    stage7()
 
     for h in range(2):
         rows = pl.ds(h * 256, 256)

time: 57.4 us -> 55.4 us (0.965)
  Pallas kernels: 56.3 us -> 54.5 us
    pallas_call x1, Pallas kernels: 55.5 us -> 53.7 us  [local(): pl.pallas_call(functools.partial(kernel, tokens), out_shape=tuple((pltpu....]
where the time goes in v5:
time: 55.4 us; the launch traced here: 55.1 us
  Pallas kernels  54.5 us (98%)
  between operations  0.64 us (1%)
    pallas_call x1, Pallas kernels, local(): pl.pallas_call(functools.partial(kernel, tokens), out_shape=tuple((pltpu....  53.7 us

profile of v5, /device:TPU:1, one launch (start us, length us, event | category | flops | bytes accessed | tf_op | source)
XLA Modules:
  0.0 55.1 jit_solution(15398418473150722533)
XLA Ops:
  0.6 53.7 %backward.1 = (bf16[512,256]{1,0:T(8,128)(2,1)S(1)}, bf16[512,256]{1,0:T(8,128)(2,1)S(1)}, f32[16,256]{1,0:T(8,128)S(1)}, f32[16,128]{1,0:T(8,128)S(1)}) custom-call(bf16[512,128]{1,0:T(8,128)(2,1)} %og.1, bf16[512,256]{1,0:T(8,128)(2,1)} %gate.1, bf16[512,256]{1,0:T(8,128)(2,1)} %up.1, s32[256,8192]{1,0:T(8,128)} %codes.1, f32[2,16384]{1,0:T(2,128)} %scales.1, ...), custom_call_target="tpu_custom_call" | custom-call | tf_op jit(solution)/shard_map/backward/pallas_call | solution.py:489
  54.3 0.8 %hand_over.1 = (bf16[512,256]{1,0:T(8,128)(2,1)}, bf16[512,256]{1,0:T(8,128)(2,1)}, f32[16,256]{1,0:T(8,128)}, f32[16,128]{1,0:T(8,128)}) custom-call(bf16[512,256]{1,0:T(8,128)(2,1)S(1)} %get-tuple-element.8.refs_0_, bf16[512,256]{1,0:T(8,128)(2,1)S(1)} %get-tuple-element.9.refs_1_, f32[16,256]{1,0:T(8,128)S(1)} %get-tuple-element.10.refs_2_, ...), custom_call_target="tpu_custom_call" | custom-call | tf_op jit(solution)/shard_map/hand_over/pallas_call | solution.py:538

commit v6 on v5

--- a/solution.py
+++ b/solution.py
@@ -17,8 +17,8 @@
 Z_SENDS = ((3, 1), (8, 3), (10, 2))
 Z_HALVES = (2, 3)
 Z_FAR = ((12, 2),)
-SOONER = (13, 17)
-CROSS_FIRST = (3, 9)
+SOONER = (11, 17)
+CROSS_FIRST = (3, 12)
 EARLY = 6
 STAGES = ((4, 1), (7, 2), (10, 3), (12, 4), (14, 5), (16, 6))
 NT = (((1,), (1,)), ((), ()))
@@ -146,6 +146,8 @@
         (0, o, me_other, neighbour(0, 0, 3, o)),
     ):
         remote(own_rows(h), buf.at[h, place_of, c], ssem, half_sem.at[i * 2 + c], dev).start()
+    for dev in (b_up, b_down):
+        remote(own_rows(c), buf.at[c, me, c], ssem, near_sem.at[pair(0, 0)], dev).start()
     local = [
         pltpu.make_async_copy(own_rows(c), buf.at[c, me, c], local_sem.at[0]),
         pltpu.make_async_copy(own_rows(o), buf.at[o, me_other, c], local_sem.at[1]),
@@ -174,7 +176,8 @@
     remote(own_rows(o), buf.at[c, me, o], sib_ssem, own_rsem.at[1], sibling).wait_recv()
     send_own_z(buf.at[c, me, o], o)
     local[0].wait()
-    send_b(0, 0, me)
+    for dev in (b_up, b_down):
+        send_half(me, o, near_sem.at[pair(0, 0)], dev)
 
     def place(s):
         da = sum(jnp.where(s == i, v[0], 0) for i, v in enumerate(ORDER) if v[0])

time: 55.4 us -> 55.4 us (level)
  no operation moved by 1% of the time
where the time goes in v6:
time: 55.4 us; the launch traced here: 55.1 us
  Pallas kernels  54.5 us (98%)
  between operations  0.64 us (1%)
    pallas_call x1, Pallas kernels, local(): pl.pallas_call(functools.partial(kernel, tokens), out_shape=tuple((pltpu....  53.7 us

profile of v6, /device:TPU:1, one launch (start us, length us, event | category | flops | bytes accessed | tf_op | source)
XLA Modules:
  0.0 55.1 jit_solution(9641306400350683080)
XLA Ops:
  0.6 53.7 %backward.1 = (bf16[512,256]{1,0:T(8,128)(2,1)S(1)}, bf16[512,256]{1,0:T(8,128)(2,1)S(1)}, f32[16,256]{1,0:T(8,128)S(1)}, f32[16,128]{1,0:T(8,128)S(1)}) custom-call(bf16[512,128]{1,0:T(8,128)(2,1)} %og.1, bf16[512,256]{1,0:T(8,128)(2,1)} %gate.1, bf16[512,256]{1,0:T(8,128)(2,1)} %up.1, s32[256,8192]{1,0:T(8,128)} %codes.1, f32[2,16384]{1,0:T(2,128)} %scales.1, ...), custom_call_target="tpu_custom_call" | custom-call | tf_op jit(solution)/shard_map/backward/pallas_call | solution.py:492
  54.3 0.8 %hand_over.1 = (bf16[512,256]{1,0:T(8,128)(2,1)}, bf16[512,256]{1,0:T(8,128)(2,1)}, f32[16,256]{1,0:T(8,128)}, f32[16,128]{1,0:T(8,128)}) custom-call(bf16[512,256]{1,0:T(8,128)(2,1)S(1)} %get-tuple-element.8.refs_0_, bf16[512,256]{1,0:T(8,128)(2,1)S(1)} %get-tuple-element.9.refs_1_, f32[16,256]{1,0:T(8,128)S(1)} %get-tuple-element.10.refs_2_, ...), custom_call_target="tpu_custom_call" | custom-call | tf_op jit(solution)/shard_map/hand_over/pallas_call | solution.py:541

commit v7 on v5

--- a/solution.py
+++ b/solution.py
@@ -17,8 +17,8 @@
 Z_SENDS = ((3, 1), (8, 3), (10, 2))
 Z_HALVES = (2, 3)
 Z_FAR = ((12, 2),)
-SOONER = (13, 17)
-CROSS_FIRST = (3, 9)
+SOONER = (11, 17)
+CROSS_FIRST = (3, 12)
 EARLY = 6
 STAGES = ((4, 1), (7, 2), (10, 3), (12, 4), (14, 5), (16, 6))
 NT = (((1,), (1,)), ((), ()))

time: 55.4 us -> 55.4 us (level)
  no operation moved by 1% of the time
where the time goes in v7:
time: 55.4 us; the launch traced here: 55.1 us
  Pallas kernels  54.5 us (98%)
  between operations  0.64 us (1%)
    pallas_call x1, Pallas kernels, local(): pl.pallas_call(functools.partial(kernel, tokens), out_shape=tuple((pltpu....  53.7 us

profile of v7, /device:TPU:1, one launch (start us, length us, event | category | flops | bytes accessed | tf_op | source)
XLA Modules:
  0.0 55.1 jit_solution(4979900572905077643)
XLA Ops:
  0.6 53.7 %backward.1 = (bf16[512,256]{1,0:T(8,128)(2,1)S(1)}, bf16[512,256]{1,0:T(8,128)(2,1)S(1)}, f32[16,256]{1,0:T(8,128)S(1)}, f32[16,128]{1,0:T(8,128)S(1)}) custom-call(bf16[512,128]{1,0:T(8,128)(2,1)} %og.1, bf16[512,256]{1,0:T(8,128)(2,1)} %gate.1, bf16[512,256]{1,0:T(8,128)(2,1)} %up.1, s32[256,8192]{1,0:T(8,128)} %codes.1, f32[2,16384]{1,0:T(2,128)} %scales.1, ...), custom_call_target="tpu_custom_call" | custom-call | tf_op jit(solution)/shard_map/backward/pallas_call | solution.py:489
  54.3 0.8 %hand_over.1 = (bf16[512,256]{1,0:T(8,128)(2,1)}, bf16[512,256]{1,0:T(8,128)(2,1)}, f32[16,256]{1,0:T(8,128)}, f32[16,128]{1,0:T(8,128)}) custom-call(bf16[512,256]{1,0:T(8,128)(2,1)S(1)} %get-tuple-element.8.refs_0_, bf16[512,256]{1,0:T(8,128)(2,1)S(1)} %get-tuple-element.9.refs_1_, f32[16,256]{1,0:T(8,128)S(1)} %get-tuple-element.10.refs_2_, ...), custom_call_target="tpu_custom_call" | custom-call | tf_op jit(solution)/shard_map/hand_over/pallas_call | solution.py:538
